TPU v7x, 32 devices: a whole 2x2x4 slice. The times are simulated.
32 devices in a mesh: tm: 8 (over z, x), mp: 4 (over y, core).
Axes of the slice: x: 2, y: 2, z: 4, core: 2. Of those that a mesh axis runs over, the one named last changes fastest.
Arguments:
- frames: bfloat16 [1536, 4096], P('mp', 'tm'), may hold values from -40 to 40
- norm_gain: float32 [1536], replicated, may hold values from 0.1 to 1.9
- w_qkv: bfloat16 [3, 1536, 1536], P(None, 'mp'), may hold values from -0.76546554 to 0.76546554
- w_out: bfloat16 [1536, 1536], P('mp'), may hold values from -0.15625 to 0.15625
- conv_kernel: float32 [31, 1536], P(None, 'mp'), may hold values from -1 to 1
- grad_out: bfloat16 [1536, 4096], P('mp', 'tm'), may hold values from -6 to 6
Outputs:
- block_out: bfloat16 [1536, 4096], P('mp', 'tm')
- grad_frames: bfloat16 [1536, 4096], P('mp', 'tm')
- grad_gain: float32 [1536], P('mp')
- grad_qkv: float32 [3, 1536, 1536], P(None, 'mp')
- grad_out_proj: float32 [1536, 1536], P('mp')
- grad_kernel: float32 [31, 1536], P(None, 'mp')
All inputs are finite; a program needn't handle non-finite values.
Results may differ from a plain program's by a relative error of at most 0.023.
The roundings to bfloat16 on the way count: a program that leaves them out, or rounds other values in their place, can miss the bound.
Values may be sent and summed in bfloat16 or wider, within the bound.
A program may use at most 128 MiB of HBM per device.

v0:
```python
import jax
import jax.numpy as jnp
from jax import lax
from jax.sharding import PartitionSpec as P

D = 1536
HEAD_DIM = 64


def with_halo(cells, sides, width):
    for axis, dim in sides:
        count = lax.axis_size(axis)
        ends = count - 1
        head = lax.slice_in_dim(cells, 0, width, axis=dim)
        tail = lax.slice_in_dim(cells, cells.shape[dim] - width, cells.shape[dim], axis=dim)
        cells = jnp.concatenate(
            [
                lax.ppermute(tail, axis, [(i, (i + 1) % count) for i in range(ends)]),
                cells,
                lax.ppermute(head, axis, [((i + 1) % count, i) for i in range(ends)]),
            ],
            axis=dim,
        )
    return cells


def score_grads(
    query_part, upstream_part, logsum_part, offset_part, key_part, value_part, score_scale
):
    scores = (
        jnp.einsum("qhd,khd->hqk", query_part, key_part, preferred_element_type=jnp.float32)
        * score_scale
    )
    probabilities = jnp.exp(scores - logsum_part[:, :, None])
    grad_prob = jnp.einsum(
        "qhd,khd->hqk", upstream_part, value_part, preferred_element_type=jnp.float32
    )
    grad_score = (probabilities * (grad_prob - offset_part[:, :, None])).astype(jnp.bfloat16)
    return (probabilities.astype(jnp.bfloat16), grad_score)


def shards(frames, norm_gain, w_qkv, w_out, conv_kernel, grad_out):
    own_width, row_count = frames.shape
    head_cols = w_qkv.shape[1]
    head_count = head_cols // HEAD_DIM
    score_scale = HEAD_DIM ** (-0.5)
    column_start = lax.axis_index("mp") * own_width
    gathered = lax.all_gather(frames, "mp", axis=0, tiled=True)
    inputs = gathered.T.astype(jnp.float32)
    inverse = lax.rsqrt(jnp.mean(inputs * inputs, axis=1, keepdims=True) + 1e-06)
    normed = (inputs * inverse * norm_gain).astype(jnp.bfloat16)
    qkv_rows = w_qkv.reshape(3 * head_cols, D)
    packed = jnp.einsum("td,cd->tc", normed, qkv_rows, preferred_element_type=jnp.float32).astype(
        jnp.bfloat16
    )
    packed = packed.reshape(row_count, 3, head_cols)
    queries = packed[:, 0]
    key_rows = packed[:, 1]
    values = packed[:, 2]
    keys_all, values_all = (
        lax.all_gather(key_rows, "tm", axis=0, tiled=True),
        lax.all_gather(values, "tm", axis=0, tiled=True),
    )
    key_total = keys_all.shape[0]
    block_size = min(512, key_total)
    block_count = key_total // block_size
    query_heads = queries.reshape(row_count, head_count, HEAD_DIM)

    def key_window(first_row):
        key_part = lax.dynamic_slice_in_dim(keys_all, first_row, block_size, 0)
        value_part = lax.dynamic_slice_in_dim(values_all, first_row, block_size, 0)
        return (
            key_part.reshape(block_size, head_count, HEAD_DIM),
            value_part.reshape(block_size, head_count, HEAD_DIM),
        )

    def forward_step(state, step_index):
        running_max, total_weight, accumulated = state
        key_part, value_part = key_window(step_index * block_size)
        scores = (
            jnp.einsum("qhd,khd->hqk", query_heads, key_part, preferred_element_type=jnp.float32)
            * score_scale
        )
        new_max = jnp.maximum(running_max, jnp.max(scores, axis=2))
        weights = jnp.exp(scores - new_max[:, :, None])
        factor = jnp.exp(running_max - new_max)
        total_weight = total_weight * factor + jnp.sum(weights, axis=2)
        accumulated = accumulated * factor[:, :, None] + jnp.einsum(
            "hqk,khd->hqd",
            weights.astype(jnp.bfloat16),
            value_part,
            preferred_element_type=jnp.float32,
        )
        return ((new_max, total_weight, accumulated), None)

    start_state = (
        jnp.full((head_count, row_count), -1e30, jnp.float32),
        jnp.zeros((head_count, row_count), jnp.float32),
        jnp.zeros((head_count, row_count, HEAD_DIM), jnp.float32),
    )
    (running_max, total_weight, accumulated), unused_out = lax.scan(
        forward_step, start_state, jnp.arange(block_count)
    )
    attended = (accumulated / total_weight[:, :, None]).astype(jnp.bfloat16)
    logsum = running_max + jnp.log(total_weight)
    attn_flat = attended.transpose(1, 0, 2).reshape(row_count, head_cols)
    projected = jnp.dot(attn_flat, w_out, preferred_element_type=jnp.float32)
    mixed_part = lax.psum_scatter(projected, "mp", scatter_dimension=1, tiled=True)
    residual_sum = (frames.astype(jnp.float32) + mixed_part.T).astype(jnp.bfloat16)
    half_width = conv_kernel.shape[0] // 2
    padded = with_halo(jnp.stack([residual_sum, grad_out]), (("tm", 2),), half_width)
    resid_pad = padded[0].astype(jnp.float32)
    upstream_pad = padded[1].astype(jnp.float32)
    resid = residual_sum.astype(jnp.float32)
    upstream = grad_out.astype(jnp.float32)
    conv_sum = jnp.zeros_like(resid)
    back_sum = upstream
    kernel_rows = []
    for tap_index in range(conv_kernel.shape[0]):
        tap_column = conv_kernel[tap_index][:, None]
        conv_sum = conv_sum + tap_column * resid_pad[:, tap_index : tap_index + row_count]
        mirror = 2 * half_width - tap_index
        back_sum = back_sum + tap_column * upstream_pad[:, mirror : mirror + row_count]
        kernel_rows.append(
            jnp.sum(upstream * resid_pad[:, tap_index : tap_index + row_count], axis=1)
        )
    block_out = (resid + conv_sum).astype(jnp.bfloat16)
    kernel_part = jnp.stack(kernel_rows)
    back_cast = back_sum.astype(jnp.bfloat16)
    back_full = lax.all_gather(back_cast, "mp", axis=0, tiled=True)
    out_proj_part = jnp.einsum(
        "tc,dt->cd", attn_flat, back_full, preferred_element_type=jnp.float32
    )
    grad_attn = jnp.einsum(
        "dt,cd->tc", back_full, w_out, preferred_element_type=jnp.float32
    ).astype(jnp.bfloat16)
    attn_heads = grad_attn.reshape(row_count, head_count, HEAD_DIM)
    offset = jnp.sum(
        attended.astype(jnp.float32) * attn_heads.astype(jnp.float32).transpose(1, 0, 2), axis=2
    )
    zero_grads = jnp.zeros((row_count, head_count, HEAD_DIM), jnp.float32)
    right_pair = jnp.stack([query_heads, attn_heads])
    pair_scale = jnp.array([score_scale, 1.0], jnp.float32)[None, :, None, None]

    def backward_step(grad_queries, step_index):
        key_part, value_part = key_window(step_index * block_size)
        probabilities, grad_score = score_grads(
            query_heads, attn_heads, logsum, offset, key_part, value_part, score_scale
        )
        grad_queries = (
            grad_queries
            + jnp.einsum("hqk,khd->qhd", grad_score, key_part, preferred_element_type=jnp.float32)
            * score_scale
        )
        left_pair = jnp.stack([grad_score, probabilities])
        pair_terms = (
            jnp.einsum("shqk,sqhd->kshd", left_pair, right_pair, preferred_element_type=jnp.float32)
            * pair_scale
        )
        return (grad_queries, pair_terms.reshape(block_size, 2 * head_cols))

    grad_queries, key_terms = lax.scan(backward_step, zero_grads, jnp.arange(block_count))
    own_grads = lax.psum_scatter(
        key_terms.reshape(key_total, 2 * head_cols), "tm", scatter_dimension=0, tiled=True
    )
    grad_keys = own_grads[:, :head_cols]
    grad_values = own_grads[:, head_cols:]
    grad_packed = jnp.stack(
        [grad_queries.reshape(row_count, head_cols), grad_keys, grad_values], axis=1
    )
    grad_packed = grad_packed.astype(jnp.bfloat16).reshape(row_count, 3 * head_cols)
    qkv_part = jnp.einsum(
        "tc,td->cd", grad_packed, normed, preferred_element_type=jnp.float32
    ).reshape(3, head_cols, D)
    grad_normed = jnp.dot(grad_packed, qkv_rows, preferred_element_type=jnp.float32)
    inputs_own = frames.T.astype(jnp.float32)
    gain_own = lax.dynamic_slice_in_dim(norm_gain, column_start, own_width, 0)
    summed_normed = lax.psum(grad_normed, "mp")
    average = jnp.mean(inputs * summed_normed * norm_gain, axis=1, keepdims=True)
    grad_own = lax.dynamic_slice_in_dim(summed_normed, column_start, own_width, 1)
    scaled = grad_own * gain_own
    norm_term = inverse * scaled - inputs_own * inverse**3 * average
    grad_frames = (back_sum + norm_term.T).astype(jnp.bfloat16)
    gain_part = jnp.sum(grad_own * inputs_own * inverse, axis=0)
    summed_grads = (
        lax.psum(qkv_part.astype(jnp.bfloat16), "tm").astype(jnp.float32),
        lax.psum(out_proj_part.astype(jnp.bfloat16), "tm").astype(jnp.float32),
        lax.psum(kernel_part.astype(jnp.bfloat16), "tm").astype(jnp.float32),
        lax.psum(gain_part.astype(jnp.bfloat16), "tm").astype(jnp.float32),
    )
    return (
        block_out,
        grad_frames,
        summed_grads[3],
        summed_grads[0],
        summed_grads[1],
        summed_grads[2],
    )


def solution(mesh):
    return jax.shard_map(
        shards,
        mesh=mesh,
        in_specs=(
            P("mp", "tm"),
            P(),
            P(None, "mp", None),
            P("mp", None),
            P(None, "mp"),
            P("mp", "tm"),
        ),
        out_specs=(
            P("mp", "tm"),
            P("mp", "tm"),
            P("mp"),
            P(None, "mp", None),
            P("mp", None),
            P(None, "mp"),
        ),
        check_vma=False,
    )
```

profile of v0, /device:TPU:0, one launch (start us, length us, event | category | flops | bytes accessed | tf_op | source)
XLA Modules:
  0.0 961.2 jit_solution(14710690138517774588)
XLA Ops:
  9.4 22.6 %all-gather.7.cloned.1.call-done = bf16[1536,512]{0,1:T(8,128)(2,1)} async-done(((bf16[384,512]{0,1:T(8,128)(2,1)}), bf16[1536,512]{0,1:T(8,128)(2,1)}) %all-gather.7.cloned.1.call-update) | async-done | bytes 1572880 | tf_op jit(solution)/shard_map/all_gather | solution.py:48
  34.8 4.7 convolution_convert_fusion.1
  45.0 62.4 %all-gather.13.cloned.1.call-done = bf16[4096,1,384]{0,2,1:T(8,128)(2,1)} async-done(((bf16[512,1,384]{0,2,1:T(8,128)(2,1)}), bf16[4096,1,384]{0,2,1:T(8,128)(2,1)}) %all-gather.13.cloned.1.call-update) | async-done | bytes 3145744 | tf_op jit(solution)/shard_map/all_gather | solution.py:62
  107.4 63.3 %all-gather.11.cloned.1.call-done = bf16[4096,1,384]{0,2,1:T(8,128)(2,1)} async-done(((bf16[512,1,384]{0,2,1:T(8,128)(2,1)}), bf16[4096,1,384]{0,2,1:T(8,128)(2,1)}) %all-gather.11.cloned.1.call-update) | async-done | bytes 3145744 | tf_op jit(solution)/shard_map/all_gather | solution.py:61
  171.2 67.9 %while.29 = (s32[]{:T(128)}, f32[6,512]{1,0:T(8,128)S(1)}, f32[6,512]{1,0:T(8,128)}, f32[6,512,64]{1,2,0:T(8,128)}, s32[8]{0:T(128)}, /*index=5*/bf16[4096,384]{...) while((s32[]{:T(128)}, f32[6,512]{1,0:T(8,128)S(1)}, ...), condition=%wide.region_4.5_spmd.clone, body=%wide.region_1.4_spmd.clone.sunk | while | flops 415841280 | bytes 29786420 | solution.py:101
  241.1 3.9 fusion.114
  248.9 32.4 %reduce-scatter.3.cloned.1.call-done = f32[512,384]{1,0:T(8,128)} async-done(((f32[512,1536]{1,0:T(8,128)}), f32[512,384]{1,0:T(8,128)}) %reduce-scatter.3.cloned.1.call-update) | async-done | bytes 786448 | tf_op jit(solution)/shard_map/reduce_scatter | solution.py:108
  283.6 3.4 collective-permute-start
  289.4 3.2 collective-permute-done.1
  295.1 3.9 fusion.110
  300.1 18.8 %all-gather.9.cloned.1.call-done = bf16[1536,512]{0,1:T(8,128)(2,1)} async-done(((bf16[384,512]{0,1:T(8,128)(2,1)}), bf16[1536,512]{0,1:T(8,128)(2,1)}) %all-gather.9.cloned.1.call-update) | async-done | bytes 1572880 | tf_op jit(solution)/shard_map/all_gather | solution.py:130
  324.0 165.7 %while.30 = (s32[]{:T(128)}, f32[512,6,64]{0,2,1:T(8,128)}, f32[8,512,768]{2,1,0:T(8,128)}, s32[8]{0:T(128)}, bf16[4096,384]{0,1:T(8,128)(2,1)}, /*index=5*/bf16...) while((s32[]{:T(128)}, f32[512,6,64]{0,2,1:T(8,128)}, ...), condition=%wide.region_8.9_spmd.clone.clone, body=%wide.region_7.8_spmd.clone.clone.sunk | while | flops 1023344640 | bytes 73617880 | solution.py:162
  333.5 3.0 fusion.170
  336.5 3.1 copy.79
  339.6 3.7 fusion.168
  354.0 3.0 fusion.170
  357.0 3.1 copy.79
  360.1 3.8 fusion.168
  374.7 3.0 fusion.170
  377.8 3.1 copy.79
  380.8 3.8 fusion.168
  395.4 3.0 fusion.170
  398.5 3.1 copy.79
  401.6 3.8 fusion.168
  416.2 3.0 fusion.170
  419.2 3.1 copy.79
  422.3 3.8 fusion.168
  436.9 3.0 fusion.170
  440.0 3.1 copy.79
  443.0 3.8 fusion.168
  457.7 3.0 fusion.170
  460.8 3.1 copy.79
  463.8 3.8 fusion.168
  478.5 3.0 fusion.170
  481.5 3.1 copy.79
  484.6 3.8 fusion.168
  491.8 205.4 %reduce-scatter.5.cloned.1.call-done = f32[512,768]{1,0:T(8,128)} async-done(((f32[4096,768]{1,0:T(8,128)}), f32[512,768]{1,0:T(8,128)}) %reduce-scatter.5.cloned.1.call-update) | async-done | bytes 1572880 | tf_op jit(solution)/shard_map/reduce_scatter | solution.py:163
  699.5 4.9 convolution_bitcast_fusion
  704.8 3.4 convolution_convert_fusion.2
  711.9 5.7 convolution_convert_fusion
  719.0 17.9 %add_convert_fusion = bf16[384,512]{0,1:T(8,128)(2,1)} fusion(f32[384,542]{0,1:T(8,128)} %get-tuple-element.387, f32[384]{0:T(512)} %copy-done.61, f32[384]{0:T(512)} %copy-done.62, f32[384]{0:T(512)S(1)} %copy-done.31, f32[384]{0:T(512)S(1)} %copy-done.33, f32[384]{0:T(512)S(1)} %copy-done.35, f32[384]{0:T(512)} %get-tuple-element.302, ...), kind=kLoop, calls=%fused_computation.192 | loop fusion | flops 13172736 | bytes 25999872 | tf_op jit(solution)/shard_map/convert_element_type | solution.py:127
  738.8 7.7 fusion.97
  766.0 5.3 stack.196
  774.1 40.0 %all-reduce = (bf16[384]{0:T(512)(128)(2,1)}, bf16[31,384]{1,0:T(8,128)(2,1)}) all-reduce(bf16[384]{0:T(512)(128)(2,1)} %fusion.41, bf16[31,384]{1,0:T(8,128)(2,1)} %stack.196), channel_id=1, replica_groups=mesh['tm'=8,'mp'=4] {'tm'}, use_global_device_ids=true, to_apply=%region_13.14 | all-reduce | flops 12288 | bytes 49152 | tf_op jit(solution)/shard_map/psum | solution.py:189
  815.4 2.9 fusion.30
  823.9 123.4 %all-reduce.7.cloned.1.call-done = (bf16[3,384,1536]{2,1,0:T(8,128)(2,1)}, bf16[384,1536]{1,0:T(8,128)(2,1)}) async-done(((bf16[3,384,1536]{2,1,0:T(8,128)(2,1)}, bf16[384,1536]{1,0:T(8,128)(2,1)}), (bf16[3,384,1536]{2,1,0:T(8,128)(2,1)}, bf16[384,1536]{1,0:T(8,128)(2,1)})) %all-reduce.7.cloned.1.call-update) | async-done | bytes 4718608 | tf_op jit(solution)/shard_map/psum | solution.py:186
  947.3 3.1 convert_element_type.127
  950.4 3.9 convert_element_type.125
  (493 shorter events, 212.6 us)
Async XLA Ops:
  7.2 27.1 %copy-start = (bf16[3,384,1536]{2,1,0:T(8,128)(2,1)S(1)}, bf16[3,384,1536]{2,1,0:T(8,128)(2,1)}, u32[]{:S(2)}) copy-start(bf16[3,384,1536]{2,1,0:T(8,128)(2,1)} %param.13) | copy-start | bytes 10616836
  7.2 24.8 %all-gather.7.cloned.1.call-start = ((), (), s32[]{:S(2)}) async-start(), calls=%async_computation.2 | async-start | bytes 1966080 | tf_op jit(solution)/shard_map/all_gather | solution.py:48
  9.3 98.1 %all-gather.13.cloned.1.call-start = ((), (), s32[]{:S(2)}) async-start(), calls=%async_computation.8 | async-start | bytes 3538944 | tf_op jit(solution)/shard_map/all_gather | solution.py:62
  44.2 126.5 %all-gather.11.cloned.1.call-start = ((), (), s32[]{:S(2)}) async-start(), calls=%async_computation.7 | async-start | bytes 3538944 | tf_op jit(solution)/shard_map/all_gather | solution.py:61
  44.9 236.4 %reduce-scatter.3.cloned.1.call-start = ((), (), s32[]{:S(2)}) async-start(), calls=%async_computation.3 | async-start | bytes 3932160 | tf_op jit(solution)/shard_map/reduce_scatter | solution.py:108
  245.1 73.9 %all-gather.9.cloned.1.call-start = ((), (), s32[]{:S(2)}) async-start(), calls=%async_computation.4 | async-start | bytes 1966080 | tf_op jit(solution)/shard_map/all_gather | solution.py:130
  248.9 46.0 %copy-start.28 = (f32[384]{0:T(512)}, f32[384]{0:T(512)S(1)}, u32[]{:S(2)}) copy-start(f32[384]{0:T(512)S(1)} %get-tuple-element.298) | copy-start | bytes 4612
  248.9 46.0 %copy-start.30 = (f32[384]{0:T(512)}, f32[384]{0:T(512)S(1)}, u32[]{:S(2)}) copy-start(f32[384]{0:T(512)S(1)} %get-tuple-element.299) | copy-start | bytes 4612
  248.9 46.0 %copy-start.32 = (f32[384]{0:T(512)}, f32[384]{0:T(512)S(1)}, u32[]{:S(2)}) copy-start(f32[384]{0:T(512)S(1)} %get-tuple-element.300) | copy-start | bytes 4612
  248.9 46.0 %copy-start.34 = (f32[384]{0:T(512)}, f32[384]{0:T(512)S(1)}, u32[]{:S(2)}) copy-start(f32[384]{0:T(512)S(1)} %get-tuple-element.301) | copy-start | bytes 4612
  281.3 13.6 %copy-start.11 = (bf16[384,512]{0,1:T(8,128)(2,1)S(1)}, bf16[384,512]{0,1:T(8,128)(2,1)}, u32[]{:S(2)}) copy-start(bf16[384,512]{0,1:T(8,128)(2,1)} %copy.32) | copy-start | bytes 1179652
  281.3 13.6 %copy-start.36 = (f32[384]{0:T(512)S(1)}, f32[384]{0:T(512)}, u32[]{:S(2)}) copy-start(f32[384]{0:T(512)} %get-tuple-element.302) | copy-start | bytes 4612
  281.3 13.6 %copy-start.37 = (f32[384]{0:T(512)S(1)}, f32[384]{0:T(512)}, u32[]{:S(2)}) copy-start(f32[384]{0:T(512)} %get-tuple-element.303) | copy-start | bytes 4612
  281.3 13.6 %copy-start.38 = (f32[384]{0:T(512)S(1)}, f32[384]{0:T(512)}, u32[]{:S(2)}) copy-start(f32[384]{0:T(512)} %get-tuple-element.304) | copy-start | bytes 4612
  281.4 13.6 %copy-start.39 = (f32[384]{0:T(512)S(1)}, f32[384]{0:T(512)}, u32[]{:S(2)}) copy-start(f32[384]{0:T(512)} %get-tuple-element.305) | copy-start | bytes 4612
  281.4 13.6 %copy-start.40 = (f32[384]{0:T(512)S(1)}, f32[384]{0:T(512)}, u32[]{:S(2)}) copy-start(f32[384]{0:T(512)} %get-tuple-element.306) | copy-start | bytes 4612
  281.4 13.6 %copy-start.41 = (f32[384]{0:T(512)S(1)}, f32[384]{0:T(512)}, u32[]{:S(2)}) copy-start(f32[384]{0:T(512)} %get-tuple-element.307) | copy-start | bytes 4612
  281.4 13.6 %copy-start.42 = (f32[384]{0:T(512)S(1)}, f32[384]{0:T(512)}, u32[]{:S(2)}) copy-start(f32[384]{0:T(512)} %get-tuple-element.308) | copy-start | bytes 4612
  281.4 13.6 %copy-start.43 = (f32[384]{0:T(512)S(1)}, f32[384]{0:T(512)}, u32[]{:S(2)}) copy-start(f32[384]{0:T(512)} %get-tuple-element.309) | copy-start | bytes 4612
  281.4 13.6 %copy-start.44 = (f32[384]{0:T(512)S(1)}, f32[384]{0:T(512)}, u32[]{:S(2)}) copy-start(f32[384]{0:T(512)} %get-tuple-element.310) | copy-start | bytes 4612
  281.4 13.6 %copy-start.45 = (f32[384]{0:T(512)S(1)}, f32[384]{0:T(512)}, u32[]{:S(2)}) copy-start(f32[384]{0:T(512)} %get-tuple-element.311) | copy-start | bytes 4612
  281.4 13.6 %copy-start.46 = (f32[384]{0:T(512)S(1)}, f32[384]{0:T(512)}, u32[]{:S(2)}) copy-start(f32[384]{0:T(512)} %get-tuple-element.312) | copy-start | bytes 4612
  281.4 13.6 %copy-start.47 = (f32[384]{0:T(512)S(1)}, f32[384]{0:T(512)}, u32[]{:S(2)}) copy-start(f32[384]{0:T(512)} %get-tuple-element.313) | copy-start | bytes 4612
  281.4 13.6 %copy-start.48 = (f32[384]{0:T(512)S(1)}, f32[384]{0:T(512)}, u32[]{:S(2)}) copy-start(f32[384]{0:T(512)} %get-tuple-element.314) | copy-start | bytes 4612
  281.4 13.6 %copy-start.49 = (f32[384]{0:T(512)S(1)}, f32[384]{0:T(512)}, u32[]{:S(2)}) copy-start(f32[384]{0:T(512)} %get-tuple-element.315) | copy-start | bytes 4612
  281.5 13.6 %copy-start.50 = (f32[384]{0:T(512)S(1)}, f32[384]{0:T(512)}, u32[]{:S(2)}) copy-start(f32[384]{0:T(512)} %get-tuple-element.316) | copy-start | bytes 4612
  283.6 5.8 collective-permute-start
  286.9 5.7 collective-permute-start.1
  289.3 9.7 %copy-start.51 = (f32[384]{0:T(512)}, f32[384]{0:T(512)S(1)}, u32[]{:S(2)}) copy-start(f32[384]{0:T(512)S(1)} %get-tuple-element.317) | copy-start | bytes 4612
  289.3 9.7 %copy-start.52 = (f32[384]{0:T(512)}, f32[384]{0:T(512)S(1)}, u32[]{:S(2)}) copy-start(f32[384]{0:T(512)S(1)} %get-tuple-element.318) | copy-start | bytes 4612
  289.3 9.7 %copy-start.53 = (f32[384]{0:T(512)}, f32[384]{0:T(512)S(1)}, u32[]{:S(2)}) copy-start(f32[384]{0:T(512)S(1)} %get-tuple-element.319) | copy-start | bytes 4612
  289.3 9.7 %copy-start.54 = (f32[384]{0:T(512)}, f32[384]{0:T(512)S(1)}, u32[]{:S(2)}) copy-start(f32[384]{0:T(512)S(1)} %get-tuple-element.320) | copy-start | bytes 4612
  289.3 9.7 %copy-start.55 = (f32[384]{0:T(512)}, f32[384]{0:T(512)S(1)}, u32[]{:S(2)}) copy-start(f32[384]{0:T(512)S(1)} %get-tuple-element.321) | copy-start | bytes 4612
  289.3 9.7 %copy-start.56 = (f32[384]{0:T(512)}, f32[384]{0:T(512)S(1)}, u32[]{:S(2)}) copy-start(f32[384]{0:T(512)S(1)} %get-tuple-element.322) | copy-start | bytes 4612
  289.3 9.7 %copy-start.57 = (f32[384]{0:T(512)}, f32[384]{0:T(512)S(1)}, u32[]{:S(2)}) copy-start(f32[384]{0:T(512)S(1)} %get-tuple-element.323) | copy-start | bytes 4612
  289.4 9.7 %copy-start.58 = (f32[384]{0:T(512)}, f32[384]{0:T(512)S(1)}, u32[]{:S(2)}) copy-start(f32[384]{0:T(512)S(1)} %get-tuple-element.324) | copy-start | bytes 4612
  289.4 9.7 %copy-start.59 = (f32[384]{0:T(512)}, f32[384]{0:T(512)S(1)}, u32[]{:S(2)}) copy-start(f32[384]{0:T(512)S(1)} %get-tuple-element.325) | copy-start | bytes 4612
  289.4 9.7 %copy-start.60 = (f32[384]{0:T(512)}, f32[384]{0:T(512)S(1)}, u32[]{:S(2)}) copy-start(f32[384]{0:T(512)S(1)} %get-tuple-element.326) | copy-start | bytes 4612
  289.4 9.7 %copy-start.61 = (f32[384]{0:T(512)}, f32[384]{0:T(512)S(1)}, u32[]{:S(2)}) copy-start(f32[384]{0:T(512)S(1)} %get-tuple-element.327) | copy-start | bytes 4612
  289.4 9.7 %copy-start.62 = (f32[384]{0:T(512)}, f32[384]{0:T(512)S(1)}, u32[]{:S(2)}) copy-start(f32[384]{0:T(512)S(1)} %get-tuple-element.328) | copy-start | bytes 4612
  299.1 398.1 %reduce-scatter.5.cloned.1.call-start = ((), (), s32[]{:S(2)}) async-start(), calls=%async_computation.5 | async-start | bytes 14155776 | tf_op jit(solution)/shard_map/reduce_scatter | solution.py:163
  489.7 282.4 %all-reduce.5.cloned.1.call-start = ((), (), s32[]{:S(2)}) async-start(), calls=%async_computation.6 | async-start | bytes 6291456 | tf_op jit(solution)/shard_map/psum | solution.py:178
  704.5 242.9 %all-reduce.7.cloned.1.call-start = ((), (), s32[]{:S(2)}) async-start(), calls=%async_computation.9 | async-start | bytes 9437184 | tf_op jit(solution)/shard_map/psum | solution.py:186
  738.8 8.3 copy-start.1
  738.8 8.3 copy-start.12
  747.0 25.1 %copy-start.65 = (f32[512]{0:T(512)S(1)}, f32[512]{0:T(512)}, u32[]{:S(2)}) copy-start(f32[512]{0:T(512)} %copy-done.63) | copy-start | bytes 6148
  747.0 68.4 %copy-start.67 = (f32[1536]{0:T(1024)S(1)}, f32[1536]{0:T(1024)}, u32[]{:S(2)}) copy-start(f32[1536]{0:T(1024)} %param.12) | copy-start | bytes 18436
  748.9 69.5 %copy-start.68 = (f32[512]{0:T(512)S(1)}, f32[512]{0:T(512)}, u32[]{:S(2)}) copy-start(f32[512]{0:T(512)} %get-tuple-element.390) | copy-start | bytes 6148
  (109 other events, 201.1 us)
Sparse Core Ops, SparseCore 0:
  9.6 22.3 all-gather.6
  44.3 63.0 all-gather.12
  109.4 61.2 all-gather.10
  245.2 36.1 reduce-scatter.2
  299.3 19.6 all-gather.8
  489.8 207.3 reduce-scatter.4
  704.6 67.5 all-reduce.4
  776.8 170.4 all-reduce.6
where the time goes:
time: 964 us; the launch traced here: 961 us
  waiting for transfers between devices  533 us (55%)
  local copies, waits for them, and re-layouts  141 us (15%)
  matrix products  138 us (14%)
  other arithmetic  76.6 us (8%)
  blocking collectives  40 us (4%)
  between operations  14.8 us (2%)
  loops' own time  11.8 us (1%)
    reduce_scatter x1, waiting for transfers between devices, shards(): lax.psum_scatter(key_terms.reshape(key_total, 2 * head_cols), 'tm', scatt...  205 us
    psum x1, waiting for transfers between devices, shards(): lax.psum(qkv_part.astype(jnp.bfloat16), 'tm').astype(jnp.float32)  123 us
    all_gather x1, waiting for transfers between devices, shards(): lax.all_gather(key_rows, 'tm', axis=0, tiled=True)  63.3 us
    all_gather x1, waiting for transfers between devices, shards(): lax.all_gather(values, 'tm', axis=0, tiled=True)  62.4 us
    psum x1, blocking collectives, shards(): lax.psum(gain_part.astype(jnp.bfloat16), 'tm').astype(jnp.float32)  40 us
    dynamic_update_slice x16, local copies, waits for them, and re-layouts, shards(): lax.scan(backward_step, zero_grads, jnp.arange(block_count))  34.8 us
    reduce_scatter x1, waiting for transfers between devices, shards(): lax.psum_scatter(projected, 'mp', scatter_dimension=1, tiled=True)  32.4 us
    dot_general x8, matrix products, backward_step(): jnp.einsum('hqk,khd->qhd', grad_score, key_part, preferred_element_type=j...  30.6 us
  transfers between devices with their start and end apart: 10, of which 9 were waited for; matrix products, arithmetic and copies ran while one was open for 9% of the time, Pallas kernels for 0%

commit v1 on v0

v1 whole, which is shorter than its diff:
```python
import functools

import jax
import jax.numpy as jnp
from jax import lax
from jax.experimental import pallas as pl
from jax.experimental.pallas import tpu as pltpu
from jax.sharding import PartitionSpec as P

HEAD_DIM = 64
VMEM_LIMIT = 52 * 1024 * 1024
F32 = jnp.float32
BF16 = jnp.bfloat16


def dot(a, b):
    return jnp.dot(a, b, preferred_element_type=F32)


def greet(n, stride):
    tm = lax.axis_index("tm")
    lane, me = tm % stride, tm // stride
    barrier = pltpu.get_barrier_semaphore()
    for k in range(1, n):
        peer = ((me + k) % n) * stride + lane
        pl.semaphore_signal(
            barrier, inc=1, device_id={"tm": peer}, device_id_type=pl.DeviceIdType.MESH
        )
    pl.semaphore_wait(barrier, n - 1)
    return lane, me


def attend_kernel(n, stride, q_ref, kv_ref, o_ref, lse_ref, all_ref, m_ref, l_ref, acc_ref, send_sem, recv_sem):
    heads, _, rows = q_ref.shape
    chunk = min(512, rows)
    lane, me = greet(n, stride)

    def block_copy(k, h, slot):
        return pltpu.make_async_remote_copy(
            src_ref=kv_ref.at[h],
            dst_ref=all_ref.at[slot, h],
            send_sem=send_sem.at[k - 1, h],
            recv_sem=recv_sem.at[k - 1, h],
            device_id={"tm": ((me + n - k) % n) * stride + lane},
            device_id_type=pl.DeviceIdType.MESH,
        )

    for k in range(1, n):
        for h in range(heads):
            block_copy(k, h, me).start()
    all_ref[me] = kv_ref[...]
    m_ref[...] = jnp.full(m_ref.shape, -1e30, F32)
    l_ref[...] = jnp.zeros(l_ref.shape, F32)
    acc_ref[...] = jnp.zeros(acc_ref.shape, F32)

    def visit(slot, h):
        q = q_ref[h]
        q_pad = jnp.concatenate([q, jnp.zeros_like(q)], axis=0)
        for c in range(rows // chunk):
            kv_t = all_ref[slot, h, :, c * chunk : (c + 1) * chunk]
            scores = dot(kv_t.T, q_pad)
            old = m_ref[h]
            new = jnp.maximum(old, jnp.max(scores, axis=0, keepdims=True))
            weights = jnp.exp(scores - new)
            factor = jnp.exp(old - new)
            m_ref[h] = new
            l_ref[h] = l_ref[h] * factor + jnp.sum(weights, axis=0, keepdims=True)
            acc_ref[h] = acc_ref[h] * factor + dot(kv_t[HEAD_DIM:], weights.astype(BF16))

    def step(i, carry):
        k, h = i // heads, i % heads

        @pl.when(k > 0)
        def _():
            block_copy(k, h, (me + k) % n).wait_recv()

        visit((me + k) % n, h)
        return carry

    lax.fori_loop(0, n * heads, step, 0)
    o_ref[...] = (acc_ref[...] / l_ref[...]).astype(BF16)
    lse_ref[...] = m_ref[...] + jnp.log(l_ref[...])
    for k in range(1, n):
        for h in range(heads):
            block_copy(k, h, me).wait_send()


def attend(n, stride, q, kv):
    heads, _, rows = q.shape
    vmem = pl.BlockSpec(memory_space=pltpu.VMEM)
    work = n * heads * rows * rows
    return pl.pallas_call(
        functools.partial(attend_kernel, n, stride),
        out_shape=(
            jax.ShapeDtypeStruct(q.shape, BF16),
            jax.ShapeDtypeStruct((heads, 1, rows), F32),
            jax.ShapeDtypeStruct((n, *kv.shape), BF16),
        ),
        in_specs=[vmem] * 2,
        out_specs=(vmem,) * 3,
        scratch_shapes=[
            pltpu.VMEM((heads, 1, rows), F32),
            pltpu.VMEM((heads, 1, rows), F32),
            pltpu.VMEM((heads, HEAD_DIM, rows), F32),
            pltpu.SemaphoreType.DMA((n - 1, heads)),
            pltpu.SemaphoreType.DMA((n - 1, heads)),
        ],
        cost_estimate=pl.CostEstimate(flops=work * 4 * HEAD_DIM, bytes_accessed=8 * kv.size * n, transcendentals=work),
        compiler_params=pltpu.CompilerParams(collective_id=0, has_side_effects=True, vmem_limit_bytes=VMEM_LIMIT),
        name="attend",
    )(q, kv)


def attend_grad_kernel(
    n, stride, q_ref, all_ref, up_ref, lse_ref, off_ref,
    dq_ref, dkv_ref, q_pad, up_pad, q_rows, up_rows, dq_acc, own, out_buf, in_buf, send_sem, recv_sem,
):
    heads, _, rows = q_ref.shape
    chunk = min(512, rows)
    lane, me = greet(n, stride)
    dq_acc[...] = jnp.zeros(dq_acc.shape, F32)

    def prepare(h, carry):
        q, up = q_ref[h], up_ref[h]
        blank = jnp.zeros_like(q)
        low, high = jnp.concatenate([q, blank], axis=0), jnp.concatenate([blank, up], axis=0)
        q_pad[h] = low
        up_pad[h] = high
        q_rows[h] = low.T
        up_rows[h] = high.T
        return carry

    lax.fori_loop(0, heads, prepare, 0)

    def visit(slot, h, store):
        for c in range(rows // chunk):
            kv_t = all_ref[slot, h, :, c * chunk : (c + 1) * chunk]
            kv = kv_t.T
            probs = jnp.exp(dot(kv, q_pad[h]) - lse_ref[h])
            grads = (probs * (dot(kv, up_pad[h]) - off_ref[h])).astype(BF16)
            dq_acc[h] = dq_acc[h] + dot(kv_t[:HEAD_DIM], grads)
            store(c, dot(grads, q_rows[h]) + dot(probs.astype(BF16), up_rows[h]))

    def sum_copy(k, h):
        return pltpu.make_async_remote_copy(
            src_ref=out_buf.at[k - 1, h],
            dst_ref=in_buf.at[k - 1, h],
            send_sem=send_sem.at[k - 1, h],
            recv_sem=recv_sem.at[k - 1, h],
            device_id={"tm": ((me + k) % n) * stride + lane},
            device_id_type=pl.DeviceIdType.MESH,
        )

    def far(i, carry):
        k, h = i // heads + 1, i % heads

        def store(c, block):
            out_buf[k - 1, h, c * chunk : (c + 1) * chunk, :] = block.astype(BF16)

        visit((me + k) % n, h, store)
        sum_copy(k, h).start()
        return carry

    lax.fori_loop(0, (n - 1) * heads, far, 0)

    def near(h, carry):
        def store(c, block):
            own[h, c * chunk : (c + 1) * chunk, :] = block

        visit(me, h, store)
        return carry

    lax.fori_loop(0, heads, near, 0)
    dq_ref[...] = (dq_acc[...] * HEAD_DIM ** (-0.5)).astype(BF16)

    def finish(h, carry):
        total = own[h]
        for k in range(1, n):
            sum_copy(k, h).wait_recv()
            total = total + in_buf[k - 1, h].astype(F32)
        dkv_ref[h] = total.T.astype(BF16)
        for k in range(1, n):
            sum_copy(k, h).wait_send()
        return carry

    lax.fori_loop(0, heads, finish, 0)


def attend_grad(n, stride, q, kv_all, up, lse, off):
    heads, _, rows = q.shape
    vmem = pl.BlockSpec(memory_space=pltpu.VMEM)
    work = n * heads * rows * rows
    wide = 2 * HEAD_DIM
    return pl.pallas_call(
        functools.partial(attend_grad_kernel, n, stride),
        out_shape=(
            jax.ShapeDtypeStruct(q.shape, BF16),
            jax.ShapeDtypeStruct((heads, wide, rows), BF16),
        ),
        in_specs=[vmem] * 5,
        out_specs=(vmem,) * 2,
        scratch_shapes=[
            pltpu.VMEM((heads, wide, rows), BF16),
            pltpu.VMEM((heads, wide, rows), BF16),
            pltpu.VMEM((heads, rows, wide), BF16),
            pltpu.VMEM((heads, rows, wide), BF16),
            pltpu.VMEM((heads, HEAD_DIM, rows), F32),
            pltpu.VMEM((heads, rows, wide), F32),
            pltpu.VMEM((n - 1, heads, rows, wide), BF16),
            pltpu.VMEM((n - 1, heads, rows, wide), BF16),
            pltpu.SemaphoreType.DMA((n - 1, heads)),
            pltpu.SemaphoreType.DMA((n - 1, heads)),
        ],
        cost_estimate=pl.CostEstimate(flops=work * 10 * HEAD_DIM, bytes_accessed=8 * kv_all.size, transcendentals=work),
        compiler_params=pltpu.CompilerParams(collective_id=1, has_side_effects=True, vmem_limit_bytes=VMEM_LIMIT),
        name="attend_grad",
    )(q, kv_all, up, lse, off)


def swap(block):
    count = lax.axis_size("tm")
    return lax.ppermute(block, "tm", [(i, i ^ 1) for i in range(count)])


def halves(block):
    low, high = jnp.split(block, 2, axis=0)
    odd = lax.axis_index("tm") % 2 == 1
    return jnp.where(odd, high, low), jnp.where(odd, low, high)


def to_heads(block):
    keep, give = halves(block)
    return jnp.concatenate([keep, swap(give)], axis=2)


def to_rows(block):
    keep, give = jnp.split(block, 2, axis=2)
    got = swap(give)
    odd = lax.axis_index("tm") % 2 == 1
    return jnp.concatenate([jnp.where(odd, got, keep), jnp.where(odd, keep, got)], axis=0)


def with_halo(cells, width):
    count = lax.axis_size("tm")
    ends = count - 1
    return jnp.concatenate(
        [
            lax.ppermute(cells[:, -width:], "tm", [(i, i + 1) for i in range(ends)]),
            cells,
            lax.ppermute(cells[:, :width], "tm", [(i + 1, i) for i in range(ends)]),
        ],
        axis=1,
    )


def shards(frames, norm_gain, w_qkv, w_out, conv_kernel, grad_out):
    own_width, row_count = frames.shape
    head_cols, width = w_qkv.shape[1:]
    heads = head_cols // HEAD_DIM
    tm = lax.axis_size("tm")
    stride = 2 if heads % 2 == 0 and tm % 2 == 0 else 1
    n = tm // stride
    taps = conv_kernel.shape[0]
    half = taps // 2

    upstream = grad_out.astype(F32)
    upstream_pad = with_halo(grad_out, half).astype(F32)
    back_sum = upstream
    for tap in range(taps):
        mirror = 2 * half - tap
        back_sum = back_sum + conv_kernel[tap][:, None] * upstream_pad[:, mirror : mirror + row_count]
    back_cast = back_sum.astype(BF16)

    gathered = lax.all_gather(frames, "mp", axis=0, tiled=True)
    inputs = gathered.astype(F32)
    inverse = lax.rsqrt(jnp.mean(inputs * inputs, axis=0, keepdims=True) + 1e-06)
    normed = (inputs * inverse * norm_gain[:, None]).astype(BF16)
    qkv_rows = w_qkv.reshape(3 * head_cols, width)
    packed = dot(qkv_rows, normed).astype(BF16).reshape(3, heads, HEAD_DIM, row_count)
    merged = packed.transpose(1, 0, 2, 3).reshape(heads, 3 * HEAD_DIM, row_count)
    if stride == 2:
        merged = to_heads(merged)
    q = merged[:, :HEAD_DIM] * jnp.asarray(HEAD_DIM ** (-0.5), BF16)
    attended_heads, lse, kv_all = attend(n, stride, q, merged[:, HEAD_DIM:])
    back_full = lax.all_gather(back_cast, "mp", axis=0, tiled=True)
    grad_attn = dot(w_out, back_full).astype(BF16).reshape(heads, HEAD_DIM, row_count)
    if stride == 2:
        attended = to_rows(attended_heads)
        up = to_heads(grad_attn)
    else:
        attended, up = attended_heads, grad_attn
    off = jnp.sum(up.astype(F32) * attended_heads.astype(F32), axis=1, keepdims=True)
    dq, dkv = attend_grad(n, stride, q, kv_all, up, lse, off)

    attn = attended.reshape(head_cols, row_count)
    out_proj_part = jnp.einsum("ct,dt->cd", attn, back_full, preferred_element_type=F32)
    projected = jnp.einsum("cd,ct->dt", w_out, attn, preferred_element_type=F32)
    mixed = lax.psum_scatter(projected.astype(BF16), "mp", scatter_dimension=0, tiled=True)
    residual_sum = (frames.astype(F32) + mixed.astype(F32)).astype(BF16)
    resid_pad = with_halo(residual_sum, half).astype(F32)
    resid = residual_sum.astype(F32)
    conv_sum = jnp.zeros_like(resid)
    kernel_rows = []
    for tap in range(taps):
        shifted = resid_pad[:, tap : tap + row_count]
        conv_sum = conv_sum + conv_kernel[tap][:, None] * shifted
        kernel_rows.append(jnp.sum(upstream * shifted, axis=1))
    block_out = (resid + conv_sum).astype(BF16)
    kernel_part = jnp.stack(kernel_rows)

    grads = jnp.concatenate([dq, dkv], axis=1)
    if stride == 2:
        grads = to_rows(grads)
    grad_packed = (
        grads.reshape(heads, 3, HEAD_DIM, row_count).transpose(1, 0, 2, 3).reshape(3 * head_cols, row_count)
    )
    qkv_part = jnp.einsum("ct,dt->cd", grad_packed, normed, preferred_element_type=F32)
    grad_normed = jnp.einsum("cd,ct->dt", qkv_rows, grad_packed, preferred_element_type=F32)
    average = lax.psum(
        jnp.sum(inputs * grad_normed * norm_gain[:, None], axis=0, keepdims=True), "mp"
    ) / width
    grad_own = lax.psum_scatter(
        grad_normed.astype(BF16), "mp", scatter_dimension=0, tiled=True
    ).astype(F32)
    start = lax.axis_index("mp") * own_width
    gain_own = lax.dynamic_slice_in_dim(norm_gain, start, own_width, 0)
    own = frames.astype(F32)
    norm_term = inverse * (grad_own * gain_own[:, None]) - own * inverse**3 * average
    grad_frames = (back_sum + norm_term).astype(BF16)
    gain_part = jnp.sum(grad_own * own * inverse, axis=1)
    return (
        block_out,
        grad_frames,
        lax.psum(gain_part, "tm"),
        lax.psum(qkv_part.astype(BF16), "tm").astype(F32).reshape(3, head_cols, width),
        lax.psum(out_proj_part.astype(BF16), "tm").astype(F32),
        lax.psum(kernel_part, "tm"),
    )


def solution(mesh):
    return jax.shard_map(
        shards,
        mesh=mesh,
        in_specs=(
            P("mp", "tm"),
            P(),
            P(None, "mp", None),
            P("mp", None),
            P(None, "mp"),
            P("mp", "tm"),
        ),
        out_specs=(
            P("mp", "tm"),
            P("mp", "tm"),
            P("mp"),
            P(None, "mp", None),
            P("mp", None),
            P(None, "mp"),
        ),
        check_vma=False,
    )
```

time: 964 us -> 478 us (0.50)
  waiting for transfers between devices: 533 us -> 137 us
  Pallas kernels: 0 us -> 144 us
  matrix products: 138 us -> 20.3 us
  local copies, waits for them, and re-layouts: 141 us -> 53.5 us
  other arithmetic: 76.6 us -> 41 us
  starting transfers between devices: 5.39 us -> 20 us
  loops' own time: 11.8 us -> 0 us
    reduce_scatter x2 -> x0, waiting for transfers between devices: 238 us -> none  [the longest x1 205 us: shards(): lax.psum_scatter(key_terms.reshape(key_total, 2 * head_cols), 'tm', scatt...]
    pallas_call x0 -> x2, Pallas kernels: none -> 144 us  [the longest x1 81.5 us: attend(): pl.pallas_call(functools.partial(attend_kernel, n, stride), out_shape=(ja...]
    all_gather x2 -> x0, waiting for transfers between devices: 126 us -> none  [the longest x1 63.3 us: shards(): lax.all_gather(key_rows, 'tm', axis=0, tiled=True)]
    dot_general x54 -> x6, matrix products: 138 us -> 20.3 us  [the longest x2 6.62 us: dot(): return jnp.dot(a, b, preferred_element_type=F32)]
    psum x2 -> x1, waiting for transfers between devices: 124 us -> 79.6 us  [shards(): lax.psum(qkv_part.astype(BF16), 'tm').astype(F32)]
    dynamic_slice x33 -> x1, local copies, waits for them, and re-layouts: 40.1 us -> 0.78 us  [shards(): gain_own = lax.dynamic_slice_in_dim(norm_gain, start, own_width, 0)]
    dynamic_update_slice x16 -> x0, local copies, waits for them, and re-layouts: 34.8 us -> none  [shards(): lax.scan(backward_step, zero_grads, jnp.arange(block_count))]
    ppermute x2 -> x8, waiting for transfers between devices: 3.24 us -> 30.3 us  [the longest x4 30.3 us: swap(): return lax.ppermute(block, 'tm', [(i, i ^ 1) for i in range(count)])]
  transfers between devices with their start and end apart: 10 -> 13, of which waited for: 9 -> 7; matrix products, arithmetic and copies ran while one was open for 9% -> 20% of each run, Pallas kernels for 0% -> 30%
where the time goes in v1:
time: 478 us; the launch traced here: 476 us
  Pallas kernels  144 us (30%)
  waiting for transfers between devices  137 us (29%)
  local copies, waits for them, and re-layouts  53.5 us (11%)
  blocking collectives  46.8 us (10%)
  other arithmetic  41 us (9%)
  matrix products  20.3 us (4%)
  starting transfers between devices  20 us (4%)
  between operations  14.2 us (3%)
    pallas_call x1, Pallas kernels, attend(): pl.pallas_call(functools.partial(attend_kernel, n, stride), out_shape=(ja...  81.5 us
    psum x1, waiting for transfers between devices, shards(): lax.psum(qkv_part.astype(BF16), 'tm').astype(F32)  79.6 us
    pallas_call x1, Pallas kernels, attend_grad(): pl.pallas_call(functools.partial(attend_grad_kernel, n, stride), out_shap...  62.2 us
    psum x1, blocking collectives, shards(): lax.psum(gain_part, 'tm')  40.1 us
    ppermute x4, waiting for transfers between devices, swap(): return lax.ppermute(block, 'tm', [(i, i ^ 1) for i in range(count)])  30.3 us
    unnamed x7, waiting for transfers between devices  24 us
    unnamed x73, local copies, waits for them, and re-layouts  22.4 us
    another operation x32, local copies, waits for them, and re-layouts, shards(): kernel_part = jnp.stack(kernel_rows)  21.4 us
  transfers between devices with their start and end apart: 13, of which 7 were waited for; matrix products, arithmetic and copies ran while one was open for 20% of the time, Pallas kernels for 30%

profile of v1, /device:TPU:0, one launch (start us, length us, event | category | flops | bytes accessed | tf_op | source)
XLA Modules:
  0.0 476.4 jit_solution(5561247347099211856)
XLA Ops:
  7.2 2.1 copy.33
  9.4 1.9 copy.38
  11.3 1.3 fusion.81
  12.6 1.3 collective-permute-start.5
  13.9 6.1 %collective-permute-start.4 = (bf16[384,15]{0,1:T(8,128)(2,1)}, bf16[384,15]{0,1:T(8,128)(2,1)}, u32[]{:S(2)}, u32[]{:S(2)}) collective-permute-start(bf16[384,15]{0,1:T(8,128)(2,1)} %get-tuple-element.115), channel_id=1, source_target_pairs={{0,4},{4,8},{8,12},{12,16},{16,20},{20,24},{24,28},{1,5},{5,9},{9,... | collective-permute-start | bytes 34568 | tf_op jit(solution)/shard_map/ppermute | solution.py:248
  20.0 1.9 slice_reduce_fusion.30
  21.8 1.7 slice_reduce_fusion.29
  24.7 4.8 %fusion.79 = (bf16[384,512]{0,1:T(8,128)(2,1)}, f32[384,512]{0,1:T(8,128)}) fusion(f32[384,542]{0,1:T(8,128)S(1)} %maximum_convert_fusion.1, f32[384]{0:T(512)} %get-tuple-element.94, f32[384]{0:T(512)} %get-tuple-element.95, f32[384]{0:T(512)S(1)} %get-tuple-element.66, f32[384]{0:T(512)S(1)} %get-tuple-element.67, f32[384]{0:T(512)S(1)} %get-tuple-element.68, ...), kind=kLoop, calls=%fused_computation.206 | loop fusion | flops 12582912 | bytes 25999872 | tf_op jit(solution)/shard_map/convert_element_type | solution.py:272
  29.6 2.9 all-gather.3.cloned.1.call-done
  32.5 1.9 fusion
  35.6 3.3 fusion.6
  38.9 2.4 copy.35
  41.3 1.5 broadcast_select_fusion.3
  42.8 1.5 collective-permute-start
  44.3 14.1 %collective-permute-done = bf16[3,192,512]{2,1,0:T(8,128)(2,1)S(1)} collective-permute-done((bf16[3,192,512]{2,1,0:T(8,128)(2,1)S(1)}, bf16[3,192,512]{2,1,0:T(8,128)(2,1)S(1)}, u32[]{:S(2)}, u32[]{:S(2)}) %collective-permute-start) | collective-permute-done | bytes 589856 | tf_op jit(solution)/shard_map/ppermute | solution.py:222
  58.6 81.5 %attend.1 = (bf16[3,64,1024]{2,1,0:T(8,128)(2,1)S(1)}, f32[3,1,1024]{2,1,0:T(1,128)S(1)}, bf16[4,3,128,1024]{3,2,1,0:T(8,128)(2,1)}) custom-call(bf16[3,64,1024]{2,1,0:T(8,128)(2,1)S(1)} %maximum_multiply_fusion.q_ref, bf16[3,128,1024]{2,1,0:T(8,128)(2,1)S(1)} %pad_maximum_fusion.1.kv_ref), custom_call_target="tpu_custom_call" | custom-call | flops 3221225472 | bytes 12582912 | tf_op jit(solution)/shard_map/attend/pallas_call | solution.py:92
  141.6 1.5 collective-permute-start.1
  143.1 3.3 fusion.7
  146.4 1.2 collective-permute-done.1
  149.4 2.1 fusion.5
  151.5 2.6 copy.45
  155.5 1.5 collective-permute-start.6
  157.0 4.2 collective-permute-done.6
  161.5 62.2 %attend_grad.1 = (bf16[3,64,1024]{2,1,0:T(8,128)(2,1)S(1)}, bf16[3,128,1024]{2,1,0:T(8,128)(2,1)S(1)}) custom-call(bf16[3,64,1024]{2,1,0:T(8,128)(2,1)S(1)} %copy-done.5, bf16[4,3,128,1024]{3,2,1,0:T(8,128)(2,1)} %get-tuple-element.12.all_ref, bf16[3,64,1024]{2,1,0:T(8,128)(2,1)S(1)} %pad_maximum_fusion.3.up_ref, ...), custom_call_target="tpu_custom_call" | custom-call | flops 8053063680 | bytes 12582912 | tf_op jit(solution)/shard_map/attend_grad/pallas_call | solution.py:194
  223.8 1.3 collective-permute-start.7
  225.1 10.9 %collective-permute-done.7 = bf16[3,192,512]{2,1,0:T(8,128)(2,1)S(1)} collective-permute-done((bf16[3,192,512]{2,1,0:T(8,128)(2,1)S(1)}, bf16[3,192,512]{2,1,0:T(8,128)(2,1)S(1)}, u32[]{:S(2)}, u32[]{:S(2)}) %collective-permute-start.7) | collective-permute-done | bytes 589856 | tf_op jit(solution)/shard_map/ppermute | solution.py:222
  236.3 1.7 copy-done.12
  238.0 4.2 fusion.4
  242.2 2.7 copy.47
  245.0 3.5 convolution_convert_fusion.3
  248.5 4.0 convolution_convert_fusion
  253.2 6.6 %psum.35 = f32[1,512]{1,0:T(1,128)} all-reduce(f32[1,512]{1,0:T(1,128)} %bitcast.52), channel_id=1, replica_groups=mesh['tm'=8,'mp'=4] {'mp'}, use_global_device_ids=true, to_apply=%region_5.6 | all-reduce | flops 512 | bytes 4096 | tf_op jit(solution)/shard_map/psum | solution.py:319
  259.9 1.3 broadcast_multiply_fusion
  261.1 1.9 copy.46
  263.1 23.9 %reduce-scatter.9.cloned.1.call-done = bf16[384,512]{1,0:T(8,128)(2,1)} async-done(((bf16[1536,512]{1,0:T(8,128)(2,1)}), bf16[384,512]{1,0:T(8,128)(2,1)}) %reduce-scatter.9.cloned.1.call-update) | async-done | bytes 393232
  287.0 1.9 copy.48
  288.9 3.2 fusion.15
  293.5 1.3 collective-permute-start.3
  294.8 5.2 %collective-permute-start.2 = (bf16[384,15]{0,1:T(8,128)(2,1)}, bf16[384,15]{0,1:T(8,128)(2,1)}, u32[]{:S(2)}, u32[]{:S(2)}) collective-permute-start(bf16[384,15]{0,1:T(8,128)(2,1)} %get-tuple-element.117), channel_id=1, source_target_pairs={{0,4},{4,8},{8,12},{12,16},{16,20},{20,24},{24,28},{1,5},{5,9},{9,... | collective-permute-start | bytes 34568 | tf_op jit(solution)/shard_map/ppermute | solution.py:248
  299.9 1.9 copy.44
  303.9 4.9 %add_convert_fusion = bf16[384,512]{0,1:T(8,128)(2,1)} fusion(bf16[384,512]{0,1:T(8,128)(2,1)} %copy-done.10, f32[384,542]{0,1:T(8,128)S(1)} %maximum_convert_fusion, f32[384]{0:T(512)} %get-tuple-element.94, f32[384]{0:T(512)} %get-tuple-element.95, f32[384]{0:T(512)S(1)} %copy-done.20, f32[384]{0:T(512)S(1)} %copy-done.22, f32[384]{0:T(512)S(1)} %copy-done.24, ...), kind=kLoop, calls=%fused_computation.156 | loop fusion | flops 12582912 | bytes 25213440 | tf_op jit(solution)/shard_map/convert_element_type | solution.py:308
  308.8 1.9 copy.43
  310.7 9.1 %fusion.71 = (f32[384]{0:T(512)S(1)}, f32[384]{0:T(512)S(1)}, f32[384]{0:T(512)S(1)}, f32[384]{0:T(512)S(1)}, f32[384]{0:T(512)S(1)}, /*index=5*/f32[384]{0:T(51...) fusion(bf16[384,512]{0,1:T(8,128)(2,1)} %copy.38, ...), kind=kLoop, calls=%fused_computation.117 | loop fusion | flops 7267584 | bytes 14576640 | tf_op jit(solution)/shard_map/reduce_sum | solution.py:307
  337.1 5.3 %stack.127 = f32[31,384]{1,0:T(8,128)} concatenate(f32[1,384]{1,0:T(1,128)S(1)} %stack.96, f32[1,384]{1,0:T(1,128)S(1)} %stack.97, f32[1,384]{1,0:T(1,128)S(1)} %stack.98, f32[1,384]{1,0:T(1,128)} %stack.99, f32[1,384]{1,0:T(1,128)} %stack.100, f32[1,384]{1,0:T(1,128)} %stack.101, f32[1,384]{1,0:T(1,128)} %stack.102, f32[1,384]{1,0:T(1,128)} %stack.103, f32[1,384]{1,0:T(1,128)} %stack.104, ...), dimensions={0} | concatenate | bytes 95232 | tf_op jit(solution)/shard_map/stack | solution.py:309
  342.4 40.1 %all-reduce = (f32[384]{0:T(512)}, f32[31,384]{1,0:T(8,128)}) all-reduce(f32[384]{0:T(512)S(1)} %copy-done.25, f32[31,384]{1,0:T(8,128)} %stack.127), channel_id=1, replica_groups=mesh['tm'=8,'mp'=4] {'tm'}, use_global_device_ids=true, to_apply=%region_7.8 | all-reduce | flops 12288 | bytes 98304 | tf_op jit(solution)/shard_map/psum | solution.py:334
  382.5 79.6 %all-reduce.4.cloned.1.call-done = (bf16[3,384,1536]{2,1,0:T(8,128)(2,1)}, bf16[384,1536]{1,0:T(8,128)(2,1)}) async-done(((bf16[3,384,1536]{2,1,0:T(8,128)(2,1)}, bf16[384,1536]{1,0:T(8,128)(2,1)}), (bf16[3,384,1536]{2,1,0:T(8,128)(2,1)}, bf16[384,1536]{1,0:T(8,128)(2,1)})) %all-reduce.4.cloned.1.call-update) | async-done | bytes 4718608 | tf_op jit(solution)/shard_map/psum | solution.py:335
  462.1 6.0 %reshape.100 = f32[3,384,1536]{2,1,0:T(8,128)} convert(bf16[3,384,1536]{2,1,0:T(8,128)(2,1)} %get-tuple-element.98) | non-fusion elementwise | flops 1769472 | bytes 10616832 | tf_op jit(solution)/shard_map/reshape | solution.py:335
  468.2 1.7 convert_element_type.101
  (133 shorter events, 29.4 us)
Async XLA Ops:
  7.2 27.9 %copy-start = (bf16[3,384,1536]{2,1,0:T(8,128)(2,1)S(1)}, bf16[3,384,1536]{2,1,0:T(8,128)(2,1)}, u32[]{:S(2)}) copy-start(bf16[3,384,1536]{2,1,0:T(8,128)(2,1)} %param.8) | copy-start | bytes 10616836
  7.2 25.3 %all-gather.3.cloned.1.call-start = ((), (), s32[]{:S(2)}) async-start(), calls=%async_computation.2 | async-start | bytes 1966080 | tf_op jit(solution)/shard_map/all_gather | solution.py:274
  9.3 133.8 %all-gather.5.cloned.1.call-start = ((), (), s32[]{:S(2)}) async-start(), calls=%async_computation.3 | async-start | bytes 1966080 | tf_op jit(solution)/shard_map/all_gather | solution.py:285
  12.6 10.9 %collective-permute-start.5 = (bf16[384,15]{0,1:T(8,128)(2,1)}, bf16[384,15]{0,1:T(8,128)(2,1)}, u32[]{:S(2)}, u32[]{:S(2)}) collective-permute-start(bf16[384,15]{0,1:T(8,128)(2,1)} %get-tuple-element.116), channel_id=1, source_target_pairs={{4,0},{8,4},{12,8},{16,12},{20,16},{24,20},{28,24},{5,1},{9,5},{13... | collective-permute-start | bytes 34568 | tf_op jit(solution)/shard_map/ppermute | solution.py:250
  13.9 9.6 %collective-permute-start.4 = (bf16[384,15]{0,1:T(8,128)(2,1)}, bf16[384,15]{0,1:T(8,128)(2,1)}, u32[]{:S(2)}, u32[]{:S(2)}) collective-permute-start(bf16[384,15]{0,1:T(8,128)(2,1)} %get-tuple-element.115), channel_id=1, source_target_pairs={{0,4},{4,8},{8,12},{12,16},{16,20},{20,24},{24,28},{1,5},{5,9},{9,... | collective-permute-start | bytes 34568 | tf_op jit(solution)/shard_map/ppermute | solution.py:248
  21.8 7.7 %copy-start.19 = (f32[384]{0:T(512)}, f32[384]{0:T(512)S(1)}, u32[]{:S(2)}) copy-start(f32[384]{0:T(512)S(1)} %get-tuple-element.66) | copy-start | bytes 4612
  21.8 7.7 %copy-start.21 = (f32[384]{0:T(512)}, f32[384]{0:T(512)S(1)}, u32[]{:S(2)}) copy-start(f32[384]{0:T(512)S(1)} %get-tuple-element.67) | copy-start | bytes 4612
  21.8 7.7 %copy-start.23 = (f32[384]{0:T(512)}, f32[384]{0:T(512)S(1)}, u32[]{:S(2)}) copy-start(f32[384]{0:T(512)S(1)} %get-tuple-element.68) | copy-start | bytes 4612
  23.5 1.2 copy-start.8
  29.5 6.1 %copy-start.29 = (f32[1536]{0:T(1024)S(1)}, f32[1536]{0:T(1024)}, u32[]{:S(2)}) copy-start(f32[1536]{0:T(1024)} %param.7) | copy-start | bytes 18436
  29.6 231.6 %reduce-scatter.7.cloned.1.call-start = ((), (), s32[]{:S(2)}) async-start(), calls=%async_computation.4 | async-start | bytes 1966080
  32.5 3.1 copy-start.11
  35.0 0.6 copy-start.27
  42.8 15.6 %collective-permute-start = (bf16[3,192,512]{2,1,0:T(8,128)(2,1)S(1)}, bf16[3,192,512]{2,1,0:T(8,128)(2,1)S(1)}, u32[]{:S(2)}, u32[]{:S(2)}) collective-permute-start(bf16[3,192,512]{2,1,0:T(8,128)(2,1)S(1)} %bitcast.49), channel_id=1, source_target_pairs={{0,4},{4,0},{8,12},{12,8},{16,20},{20,16},{24,28},{28,24},{1,5},{5... | collective-permute-start | bytes 1769480 | tf_op jit(solution)/shard_map/ppermute | solution.py:222
  58.5 81.7 %copy-start.4 = (bf16[3,64,1024]{2,1,0:T(8,128)(2,1)}, bf16[3,64,1024]{2,1,0:T(8,128)(2,1)S(1)}, u32[]{:S(2)}) copy-start(bf16[3,64,1024]{2,1,0:T(8,128)(2,1)S(1)} %maximum_multiply_fusion.q_ref) | copy-start | bytes 1179652
  140.2 0.7 copy-start.1
  141.6 6.0 %collective-permute-start.1 = (bf16[3,64,512]{2,1,0:T(8,128)(2,1)}, bf16[3,64,512]{2,1,0:T(8,128)(2,1)}, u32[]{:S(2)}, u32[]{:S(2)}) collective-permute-start(bf16[3,64,512]{2,1,0:T(8,128)(2,1)} %split.26), channel_id=1, source_target_pairs={{0,4},{4,0},{8,12},{12,8},{16,20},{20,16},{24,28},{28,24},{1,5},{5... | collective-permute-start | bytes 589832 | tf_op jit(solution)/shard_map/ppermute | solution.py:222
  143.1 4.5 copy-start.2
  146.4 2.9 copy-start.15
  148.6 0.7 copy-start.14
  154.1 132.9 %reduce-scatter.9.cloned.1.call-start = ((), (), s32[]{:S(2)}) async-start(), calls=%async_computation.5 | async-start | bytes 1966080
  154.4 6.9 %copy-start.3 = (bf16[3,64,1024]{2,1,0:T(8,128)(2,1)S(1)}, bf16[3,64,1024]{2,1,0:T(8,128)(2,1)}, u32[]{:S(2)}) copy-start(bf16[3,64,1024]{2,1,0:T(8,128)(2,1)} %copy-done.1) | copy-start | bytes 1179652
  154.4 7.1 %copy-start.5 = (bf16[3,64,1024]{2,1,0:T(8,128)(2,1)S(1)}, bf16[3,64,1024]{2,1,0:T(8,128)(2,1)}, u32[]{:S(2)}) copy-start(bf16[3,64,1024]{2,1,0:T(8,128)(2,1)} %copy-done.4) | copy-start | bytes 1179652
  155.5 5.7 %collective-permute-start.6 = (bf16[3,64,512]{2,1,0:T(8,128)(2,1)S(1)}, bf16[3,64,512]{2,1,0:T(8,128)(2,1)S(1)}, u32[]{:S(2)}, u32[]{:S(2)}) collective-permute-start(bf16[3,64,512]{2,1,0:T(8,128)(2,1)S(1)} %bitcast.50), channel_id=1, source_target_pairs={{0,4},{4,0},{8,12},{12,8},{16,20},{20,16},{24,28},{28,24},{1,5},{5... | collective-permute-start | bytes 589832 | tf_op jit(solution)/shard_map/ppermute | solution.py:222
  223.8 12.2 %collective-permute-start.7 = (bf16[3,192,512]{2,1,0:T(8,128)(2,1)S(1)}, bf16[3,192,512]{2,1,0:T(8,128)(2,1)S(1)}, u32[]{:S(2)}, u32[]{:S(2)}) collective-permute-start(bf16[3,192,512]{2,1,0:T(8,128)(2,1)S(1)} %split.36), channel_id=1, source_target_pairs={{0,4},{4,0},{8,12},{12,8},{16,20},{20,16},{24,28},{28,24},{1,5},{5... | collective-permute-start | bytes 1769480 | tf_op jit(solution)/shard_map/ppermute | solution.py:222
  236.2 1.8 copy-start.12
  236.2 1.8 copy-start.30
  236.3 5.9 %copy-start.17 = (bf16[6,3,64,512]{3,2,0,1:T(8,128)(2,1)}, bf16[6,3,64,512]{3,2,0,1:T(8,128)(2,1)S(1)}, u32[]{:S(2)}) copy-start(bf16[6,3,64,512]{3,2,0,1:T(8,128)(2,1)S(1)} %copy.42) | copy-start | bytes 3538948
  244.9 3.6 copy-start.28
  244.9 217.3 %all-reduce.4.cloned.1.call-start = ((), (), s32[]{:S(2)}) async-start(), calls=%async_computation.6 | async-start | bytes 9437184 | tf_op jit(solution)/shard_map/psum | solution.py:335
  244.9 3.5 copy-start.13
  244.9 3.5 copy-start.18
  245.0 3.5 copy-start.31
  252.4 36.5 %copy-start.26 = (f32[512]{0:T(512)S(1)}, f32[512]{0:T(512)}, u32[]{:S(2)}) copy-start(f32[512]{0:T(512)} %get-tuple-element.119) | copy-start | bytes 6148
  292.2 0.7 copy-start.10
  292.2 11.7 %copy-start.20 = (f32[384]{0:T(512)S(1)}, f32[384]{0:T(512)}, u32[]{:S(2)}) copy-start(f32[384]{0:T(512)} %copy-done.19) | copy-start | bytes 4612
  292.2 11.7 %copy-start.22 = (f32[384]{0:T(512)S(1)}, f32[384]{0:T(512)}, u32[]{:S(2)}) copy-start(f32[384]{0:T(512)} %copy-done.21) | copy-start | bytes 4612
  292.2 11.7 %copy-start.24 = (f32[384]{0:T(512)S(1)}, f32[384]{0:T(512)}, u32[]{:S(2)}) copy-start(f32[384]{0:T(512)} %copy-done.23) | copy-start | bytes 4612
  293.5 8.4 %collective-permute-start.3 = (bf16[384,15]{0,1:T(8,128)(2,1)}, bf16[384,15]{0,1:T(8,128)(2,1)}, u32[]{:S(2)}, u32[]{:S(2)}) collective-permute-start(bf16[384,15]{0,1:T(8,128)(2,1)} %get-tuple-element.118), channel_id=1, source_target_pairs={{4,0},{8,4},{12,8},{16,12},{20,16},{24,20},{28,24},{5,1},{9,5},{13... | collective-permute-start | bytes 34568 | tf_op jit(solution)/shard_map/ppermute | solution.py:250
  294.8 7.1 %collective-permute-start.2 = (bf16[384,15]{0,1:T(8,128)(2,1)}, bf16[384,15]{0,1:T(8,128)(2,1)}, u32[]{:S(2)}, u32[]{:S(2)}) collective-permute-start(bf16[384,15]{0,1:T(8,128)(2,1)} %get-tuple-element.117), channel_id=1, source_target_pairs={{0,4},{4,8},{8,12},{12,16},{16,20},{20,24},{24,28},{1,5},{5,9},{9,... | collective-permute-start | bytes 34568 | tf_op jit(solution)/shard_map/ppermute | solution.py:248
  303.0 0.9 copy-start.6
  310.7 17.2 %copy-start.7 = (f32[384,542]{0,1:T(8,128)S(1)}, f32[384,542]{0,1:T(8,128)}, u32[]{:S(2)}) copy-start(f32[384,542]{0,1:T(8,128)} %copy-done.6) | copy-start | bytes 2497540
  310.7 17.2 %copy-start.9 = (bf16[384,512]{0,1:T(8,128)(2,1)S(1)}, bf16[384,512]{0,1:T(8,128)(2,1)}, u32[]{:S(2)}) copy-start(bf16[384,512]{0,1:T(8,128)(2,1)} %copy.38) | copy-start | bytes 1179652
  327.9 14.5 %copy-start.25 = (f32[384]{0:T(512)S(1)}, f32[384]{0:T(512)}, u32[]{:S(2)}) copy-start(f32[384]{0:T(512)} %get-tuple-element.108) | copy-start | bytes 4612
  462.1 6.1 %copy-start.16 = (bf16[384,1536]{1,0:T(8,128)(2,1)S(1)}, bf16[384,1536]{1,0:T(8,128)(2,1)}, u32[]{:S(2)}) copy-start(bf16[384,1536]{1,0:T(8,128)(2,1)} %get-tuple-element.99) | copy-start | bytes 3538948
Sparse Core Ops, SparseCore 0:
  10.2 22.3 all-gather.2
  34.1 19.6 all-gather.4
  154.2 25.3 reduce-scatter.6
  245.0 41.9 reduce-scatter.8
  291.1 171.0 all-reduce.3
